TPU v7x, 32 devices: a whole 2x2x4 slice. The times are simulated.
32 devices in a mesh: dp: 8 (over y, x, core), tensor: 4 (over z).
Axes of the slice: x: 2, y: 2, z: 4, core: 2. Of those that a mesh axis runs over, the one named last changes fastest.
Arguments:
- inputs: bfloat16 [2048, 4096], P('dp', 'tensor'), may hold values from -6 to 6
- grad_out: bfloat16 [2048, 4096], P('dp', 'tensor'), may hold values from -6 to 6
- gate_pre: bfloat16 [2048, 3584], P('dp', 'tensor'), may hold values from -6 to 6
- up_pre: bfloat16 [2048, 3584], P('dp', 'tensor'), may hold values from -6 to 6
- down_weight: bfloat16 [3584, 4096], P('tensor', 'dp'), may hold values from -0.09375 to 0.09375
- warm_start: float32 [3, 4096, 32], P(None, 'tensor'), may hold values from -6 to 6
Outputs:
- left_factor: float32 [3, 3584, 32], P(None, 'tensor')
- right_factor: float32 [3, 4096, 32], P(None, 'tensor')
All inputs are finite; a program needn't handle non-finite values.
Results may differ from a plain program's by a relative error of at most 0.003.
Values may be sent and summed in bfloat16 or wider, within the bound.
A program may use at most 64 MiB of HBM per device.

v0:
```python
import jax
import jax.numpy as jnp
from jax import lax
from jax.sharding import PartitionSpec as P


def orthonormal_columns(block):
    high = lax.Precision.HIGHEST
    columns_count = block.shape[2]

    def column_turn(column_index, basis):
        column = lax.dynamic_slice_in_dim(block, column_index, 1, 2)[:, :, 0]
        correlation = jnp.einsum("kfr,kf->kr", basis, column, precision=high)
        square = jnp.sum(column * column, axis=1)
        correlation, square = lax.psum((correlation, square), "tensor")
        remainder = column - jnp.einsum("kfr,kr->kf", basis, correlation, precision=high)
        length = jnp.sqrt(square - jnp.sum(correlation * correlation, axis=1))
        fresh = remainder / length[:, None]
        return lax.dynamic_update_slice_in_dim(basis, fresh[:, :, None], column_index, 2)

    return lax.fori_loop(0, columns_count, column_turn, jnp.zeros_like(block))


def shards(inputs, grad_out, gate_pre, up_pre, down_weight, warm_start):
    f32 = jnp.float32
    bf16 = jnp.bfloat16
    high = lax.Precision.HIGHEST
    features, upstream = (
        lax.all_gather(inputs, "tensor", axis=1, tiled=True),
        lax.all_gather(grad_out, "tensor", axis=1, tiled=True),
    )
    tokens_here = upstream.shape[0]
    gate_f = gate_pre.astype(f32)
    up_f = up_pre.astype(f32)
    sigma = jax.nn.sigmoid(gate_f)
    hidden = (gate_f * sigma * up_f).astype(bf16)
    hidden_grad = jnp.einsum(
        "tc,fc->tf",
        upstream,
        lax.all_gather(down_weight, "dp", axis=1, tiled=True),
        preferred_element_type=f32,
    )
    gate_grad = (hidden_grad * up_f * sigma * (1.0 + gate_f * (1.0 - sigma))).astype(bf16)
    up_grad = (hidden_grad * gate_f * sigma).astype(bf16)
    own_pairs = ((gate_grad, features), (up_grad, features), (hidden, upstream))
    warm_full = lax.all_gather(warm_start, "tensor", axis=1, tiled=True)
    projections = jnp.stack(
        [
            jnp.dot(own_pairs[index][1].astype(f32), warm_full[index], precision=high)
            for index in range(3)
        ]
    )
    lefts = []
    for index in range(3):
        left_part = own_pairs[index][0].astype(f32)
        lefts.append(jnp.dot(left_part.T, projections[index], precision=high) / tokens_here)
    left_raw = lax.psum(jnp.stack(lefts), "dp")
    left_factor = orthonormal_columns(left_raw)
    replicas_count = lax.axis_size("dp")
    rights = []
    for index in range(3):
        left_part = own_pairs[index][0].astype(f32)
        right_part = own_pairs[index][1].astype(f32)
        mapped = jnp.dot(left_part, left_factor[index], precision=high)
        rights.append(jnp.dot(right_part.T, mapped, precision=high) / tokens_here)
    right_local = jnp.stack(rights)
    right_full = lax.psum(right_local, ("dp", "tensor")) / replicas_count
    share = right_full.shape[1] // lax.axis_size("tensor")
    right_own = lax.dynamic_slice_in_dim(right_full, lax.axis_index("tensor") * share, share, 1)
    return (left_factor, right_own)


def solution(mesh):
    placed = (
        P("dp", "tensor"),
        P("dp", "tensor"),
        P("dp", "tensor"),
        P("dp", "tensor"),
        P("tensor", "dp"),
        P(None, "tensor", None),
    )
    return jax.shard_map(
        shards,
        mesh=mesh,
        in_specs=placed,
        out_specs=(P(None, "tensor", None), P(None, "tensor", None)),
        check_vma=False,
    )
```

profile of v0, /device:TPU:0, one launch (start us, length us, event | category | flops | bytes accessed | tf_op | source)
XLA Modules:
  0.0 767.9 jit_solution(10446520505469387835)
XLA Ops:
  10.0 39.4 %all-gather.11.cloned.1.call-done = f32[3,4096,32]{1,2,0:T(8,128)} async-done(((f32[3,1024,32]{1,2,0:T(8,128)}), f32[3,4096,32]{1,2,0:T(8,128)}) %all-gather.11.cloned.1.call-update) | async-done | bytes 1572880 | tf_op jit(solution)/shard_map/all_gather | solution.py:46
  49.4 46.4 %all-gather.9.cloned.1.call-done = bf16[256,4096]{1,0:T(8,128)(2,1)} async-done(((bf16[256,1024]{1,0:T(8,128)(2,1)}), bf16[256,4096]{1,0:T(8,128)(2,1)}) %all-gather.9.cloned.1.call-update) | async-done | bytes 2097168 | tf_op jit(solution)/shard_map/all_gather | solution.py:29
  95.8 3.7 fusion.26
  99.5 2.9 fusion.27
  102.5 39.6 %all-gather.5.cloned.1.call-done = bf16[256,4096]{1,0:T(8,128)(2,1)} async-done(((bf16[256,1024]{1,0:T(8,128)(2,1)}), bf16[256,4096]{1,0:T(8,128)(2,1)}) %all-gather.5.cloned.1.call-update) | async-done | bytes 2097168 | tf_op jit(solution)/shard_map/all_gather | solution.py:30
  142.1 4.2 fusion.25
  146.3 47.6 %all-gather.7.cloned.1.call-done = bf16[896,4096]{1,0:T(8,128)(2,1)} async-done(((bf16[896,512]{1,0:T(8,128)(2,1)}), bf16[896,4096]{1,0:T(8,128)(2,1)}) %all-gather.7.cloned.1.call-update) | async-done | bytes 7340048 | tf_op jit(solution)/shard_map/all_gather | solution.py:40
  193.9 6.5 fusion.17
  202.4 52.6 %all-reduce.6.cloned.1.call-done = f32[3,896,32]{1,2,0:T(8,128)} async-done(((f32[3,896,32]{1,2,0:T(8,128)}), f32[3,896,32]{1,2,0:T(8,128)}) %all-reduce.6.cloned.1.call-update) | async-done | bytes 344080 | tf_op jit(solution)/shard_map/psum | solution.py:57
  255.0 365.3 %while.13 = (s32[]{:T(128)}, f32[3,896,32]{1,0,2:T(4,128)S(1)}, f32[3,896,32]{1,2,0:T(8,128)}, s32[]{:T(128)}) while((s32[]{:T(128)}, f32[3,896,32]{1,0,2:T(4,128)S(1)}, f32[3,896,32]{1,2,0:T(8,128)}, s32[]{:T(128)}) %tuple.42), condition=%wide.region_6.0_spmd, body=%wide.region_1.0_spmd.sunk | while | flops 2075426 | bytes 781073 | solution.py:21
  255.0 0.9 constant_dynamic-slice_fusion.2
  256.5 11.7 %all-reduce.2 = (f32[3,32]{1,0:T(4,128)S(1)}, f32[3]{0:T(128)S(1)}) all-reduce(f32[3,32]{1,0:T(4,128)S(1)} %bitcast.93, f32[3]{0:T(128)S(1)} %fusion.71), channel_id=1, replica_groups=mesh['dp'=8,'tensor'=4] {'tensor'}, use_global_device_ids=true, to_apply=%region_2.0 | all-reduce | flops 99 | bytes 792 | tf_op jit(solution)/shard_map/while/body/eval_jaxpr/psum | solution.py:15
  268.7 0.9 constant_dynamic-slice_fusion.2
  270.2 8.4 %all-reduce.2 = (f32[3,32]{1,0:T(4,128)S(1)}, f32[3]{0:T(128)S(1)}) all-reduce(f32[3,32]{1,0:T(4,128)S(1)} %bitcast.93, f32[3]{0:T(128)S(1)} %fusion.71), channel_id=1, replica_groups=mesh['dp'=8,'tensor'=4] {'tensor'}, use_global_device_ids=true, to_apply=%region_2.0 | all-reduce | flops 99 | bytes 792 | tf_op jit(solution)/shard_map/while/body/eval_jaxpr/psum | solution.py:15
  279.1 0.9 constant_dynamic-slice_fusion.2
  280.5 10.4 %all-reduce.2 = (f32[3,32]{1,0:T(4,128)S(1)}, f32[3]{0:T(128)S(1)}) all-reduce(f32[3,32]{1,0:T(4,128)S(1)} %bitcast.93, f32[3]{0:T(128)S(1)} %fusion.71), channel_id=1, replica_groups=mesh['dp'=8,'tensor'=4] {'tensor'}, use_global_device_ids=true, to_apply=%region_2.0 | all-reduce | flops 99 | bytes 792 | tf_op jit(solution)/shard_map/while/body/eval_jaxpr/psum | solution.py:15
  291.4 0.9 constant_dynamic-slice_fusion.2
  292.9 8.4 %all-reduce.2 = (f32[3,32]{1,0:T(4,128)S(1)}, f32[3]{0:T(128)S(1)}) all-reduce(f32[3,32]{1,0:T(4,128)S(1)} %bitcast.93, f32[3]{0:T(128)S(1)} %fusion.71), channel_id=1, replica_groups=mesh['dp'=8,'tensor'=4] {'tensor'}, use_global_device_ids=true, to_apply=%region_2.0 | all-reduce | flops 99 | bytes 792 | tf_op jit(solution)/shard_map/while/body/eval_jaxpr/psum | solution.py:15
  301.8 0.9 constant_dynamic-slice_fusion.2
  303.3 10.4 %all-reduce.2 = (f32[3,32]{1,0:T(4,128)S(1)}, f32[3]{0:T(128)S(1)}) all-reduce(f32[3,32]{1,0:T(4,128)S(1)} %bitcast.93, f32[3]{0:T(128)S(1)} %fusion.71), channel_id=1, replica_groups=mesh['dp'=8,'tensor'=4] {'tensor'}, use_global_device_ids=true, to_apply=%region_2.0 | all-reduce | flops 99 | bytes 792 | tf_op jit(solution)/shard_map/while/body/eval_jaxpr/psum | solution.py:15
  314.2 0.9 constant_dynamic-slice_fusion.2
  315.6 8.4 %all-reduce.2 = (f32[3,32]{1,0:T(4,128)S(1)}, f32[3]{0:T(128)S(1)}) all-reduce(f32[3,32]{1,0:T(4,128)S(1)} %bitcast.93, f32[3]{0:T(128)S(1)} %fusion.71), channel_id=1, replica_groups=mesh['dp'=8,'tensor'=4] {'tensor'}, use_global_device_ids=true, to_apply=%region_2.0 | all-reduce | flops 99 | bytes 792 | tf_op jit(solution)/shard_map/while/body/eval_jaxpr/psum | solution.py:15
  324.5 0.9 constant_dynamic-slice_fusion.2
  326.0 10.4 %all-reduce.2 = (f32[3,32]{1,0:T(4,128)S(1)}, f32[3]{0:T(128)S(1)}) all-reduce(f32[3,32]{1,0:T(4,128)S(1)} %bitcast.93, f32[3]{0:T(128)S(1)} %fusion.71), channel_id=1, replica_groups=mesh['dp'=8,'tensor'=4] {'tensor'}, use_global_device_ids=true, to_apply=%region_2.0 | all-reduce | flops 99 | bytes 792 | tf_op jit(solution)/shard_map/while/body/eval_jaxpr/psum | solution.py:15
  336.9 0.9 constant_dynamic-slice_fusion.2
  338.4 8.4 %all-reduce.2 = (f32[3,32]{1,0:T(4,128)S(1)}, f32[3]{0:T(128)S(1)}) all-reduce(f32[3,32]{1,0:T(4,128)S(1)} %bitcast.93, f32[3]{0:T(128)S(1)} %fusion.71), channel_id=1, replica_groups=mesh['dp'=8,'tensor'=4] {'tensor'}, use_global_device_ids=true, to_apply=%region_2.0 | all-reduce | flops 99 | bytes 792 | tf_op jit(solution)/shard_map/while/body/eval_jaxpr/psum | solution.py:15
  347.3 0.9 constant_dynamic-slice_fusion.2
  348.7 10.4 %all-reduce.2 = (f32[3,32]{1,0:T(4,128)S(1)}, f32[3]{0:T(128)S(1)}) all-reduce(f32[3,32]{1,0:T(4,128)S(1)} %bitcast.93, f32[3]{0:T(128)S(1)} %fusion.71), channel_id=1, replica_groups=mesh['dp'=8,'tensor'=4] {'tensor'}, use_global_device_ids=true, to_apply=%region_2.0 | all-reduce | flops 99 | bytes 792 | tf_op jit(solution)/shard_map/while/body/eval_jaxpr/psum | solution.py:15
  359.7 0.9 constant_dynamic-slice_fusion.2
  361.1 8.4 %all-reduce.2 = (f32[3,32]{1,0:T(4,128)S(1)}, f32[3]{0:T(128)S(1)}) all-reduce(f32[3,32]{1,0:T(4,128)S(1)} %bitcast.93, f32[3]{0:T(128)S(1)} %fusion.71), channel_id=1, replica_groups=mesh['dp'=8,'tensor'=4] {'tensor'}, use_global_device_ids=true, to_apply=%region_2.0 | all-reduce | flops 99 | bytes 792 | tf_op jit(solution)/shard_map/while/body/eval_jaxpr/psum | solution.py:15
  370.1 0.9 constant_dynamic-slice_fusion.2
  371.5 10.4 %all-reduce.2 = (f32[3,32]{1,0:T(4,128)S(1)}, f32[3]{0:T(128)S(1)}) all-reduce(f32[3,32]{1,0:T(4,128)S(1)} %bitcast.93, f32[3]{0:T(128)S(1)} %fusion.71), channel_id=1, replica_groups=mesh['dp'=8,'tensor'=4] {'tensor'}, use_global_device_ids=true, to_apply=%region_2.0 | all-reduce | flops 99 | bytes 792 | tf_op jit(solution)/shard_map/while/body/eval_jaxpr/psum | solution.py:15
  382.4 0.9 constant_dynamic-slice_fusion.2
  383.9 8.4 %all-reduce.2 = (f32[3,32]{1,0:T(4,128)S(1)}, f32[3]{0:T(128)S(1)}) all-reduce(f32[3,32]{1,0:T(4,128)S(1)} %bitcast.93, f32[3]{0:T(128)S(1)} %fusion.71), channel_id=1, replica_groups=mesh['dp'=8,'tensor'=4] {'tensor'}, use_global_device_ids=true, to_apply=%region_2.0 | all-reduce | flops 99 | bytes 792 | tf_op jit(solution)/shard_map/while/body/eval_jaxpr/psum | solution.py:15
  392.8 0.9 constant_dynamic-slice_fusion.2
  394.3 10.4 %all-reduce.2 = (f32[3,32]{1,0:T(4,128)S(1)}, f32[3]{0:T(128)S(1)}) all-reduce(f32[3,32]{1,0:T(4,128)S(1)} %bitcast.93, f32[3]{0:T(128)S(1)} %fusion.71), channel_id=1, replica_groups=mesh['dp'=8,'tensor'=4] {'tensor'}, use_global_device_ids=true, to_apply=%region_2.0 | all-reduce | flops 99 | bytes 792 | tf_op jit(solution)/shard_map/while/body/eval_jaxpr/psum | solution.py:15
  405.2 0.9 constant_dynamic-slice_fusion.2
  406.6 8.4 %all-reduce.2 = (f32[3,32]{1,0:T(4,128)S(1)}, f32[3]{0:T(128)S(1)}) all-reduce(f32[3,32]{1,0:T(4,128)S(1)} %bitcast.93, f32[3]{0:T(128)S(1)} %fusion.71), channel_id=1, replica_groups=mesh['dp'=8,'tensor'=4] {'tensor'}, use_global_device_ids=true, to_apply=%region_2.0 | all-reduce | flops 99 | bytes 792 | tf_op jit(solution)/shard_map/while/body/eval_jaxpr/psum | solution.py:15
  415.5 0.9 constant_dynamic-slice_fusion.2
  417.0 10.4 %all-reduce.2 = (f32[3,32]{1,0:T(4,128)S(1)}, f32[3]{0:T(128)S(1)}) all-reduce(f32[3,32]{1,0:T(4,128)S(1)} %bitcast.93, f32[3]{0:T(128)S(1)} %fusion.71), channel_id=1, replica_groups=mesh['dp'=8,'tensor'=4] {'tensor'}, use_global_device_ids=true, to_apply=%region_2.0 | all-reduce | flops 99 | bytes 792 | tf_op jit(solution)/shard_map/while/body/eval_jaxpr/psum | solution.py:15
  429.4 8.4 %all-reduce.2 = (f32[3,32]{1,0:T(4,128)S(1)}, f32[3]{0:T(128)S(1)}) all-reduce(f32[3,32]{1,0:T(4,128)S(1)} %bitcast.93, f32[3]{0:T(128)S(1)} %fusion.71), channel_id=1, replica_groups=mesh['dp'=8,'tensor'=4] {'tensor'}, use_global_device_ids=true, to_apply=%region_2.0 | all-reduce | flops 99 | bytes 792 | tf_op jit(solution)/shard_map/while/body/eval_jaxpr/psum | solution.py:15
  439.8 10.3 %all-reduce.2 = (f32[3,32]{1,0:T(4,128)S(1)}, f32[3]{0:T(128)S(1)}) all-reduce(f32[3,32]{1,0:T(4,128)S(1)} %bitcast.93, f32[3]{0:T(128)S(1)} %fusion.71), channel_id=1, replica_groups=mesh['dp'=8,'tensor'=4] {'tensor'}, use_global_device_ids=true, to_apply=%region_2.0 | all-reduce | flops 99 | bytes 792 | tf_op jit(solution)/shard_map/while/body/eval_jaxpr/psum | solution.py:15
  452.1 8.4 %all-reduce.2 = (f32[3,32]{1,0:T(4,128)S(1)}, f32[3]{0:T(128)S(1)}) all-reduce(f32[3,32]{1,0:T(4,128)S(1)} %bitcast.93, f32[3]{0:T(128)S(1)} %fusion.71), channel_id=1, replica_groups=mesh['dp'=8,'tensor'=4] {'tensor'}, use_global_device_ids=true, to_apply=%region_2.0 | all-reduce | flops 99 | bytes 792 | tf_op jit(solution)/shard_map/while/body/eval_jaxpr/psum | solution.py:15
  462.5 10.3 %all-reduce.2 = (f32[3,32]{1,0:T(4,128)S(1)}, f32[3]{0:T(128)S(1)}) all-reduce(f32[3,32]{1,0:T(4,128)S(1)} %bitcast.93, f32[3]{0:T(128)S(1)} %fusion.71), channel_id=1, replica_groups=mesh['dp'=8,'tensor'=4] {'tensor'}, use_global_device_ids=true, to_apply=%region_2.0 | all-reduce | flops 99 | bytes 792 | tf_op jit(solution)/shard_map/while/body/eval_jaxpr/psum | solution.py:15
  474.8 8.4 %all-reduce.2 = (f32[3,32]{1,0:T(4,128)S(1)}, f32[3]{0:T(128)S(1)}) all-reduce(f32[3,32]{1,0:T(4,128)S(1)} %bitcast.93, f32[3]{0:T(128)S(1)} %fusion.71), channel_id=1, replica_groups=mesh['dp'=8,'tensor'=4] {'tensor'}, use_global_device_ids=true, to_apply=%region_2.0 | all-reduce | flops 99 | bytes 792 | tf_op jit(solution)/shard_map/while/body/eval_jaxpr/psum | solution.py:15
  485.2 10.3 %all-reduce.2 = (f32[3,32]{1,0:T(4,128)S(1)}, f32[3]{0:T(128)S(1)}) all-reduce(f32[3,32]{1,0:T(4,128)S(1)} %bitcast.93, f32[3]{0:T(128)S(1)} %fusion.71), channel_id=1, replica_groups=mesh['dp'=8,'tensor'=4] {'tensor'}, use_global_device_ids=true, to_apply=%region_2.0 | all-reduce | flops 99 | bytes 792 | tf_op jit(solution)/shard_map/while/body/eval_jaxpr/psum | solution.py:15
  497.6 8.5 %all-reduce.2 = (f32[3,32]{1,0:T(4,128)S(1)}, f32[3]{0:T(128)S(1)}) all-reduce(f32[3,32]{1,0:T(4,128)S(1)} %bitcast.93, f32[3]{0:T(128)S(1)} %fusion.71), channel_id=1, replica_groups=mesh['dp'=8,'tensor'=4] {'tensor'}, use_global_device_ids=true, to_apply=%region_2.0 | all-reduce | flops 99 | bytes 792 | tf_op jit(solution)/shard_map/while/body/eval_jaxpr/psum | solution.py:15
  508.0 10.3 %all-reduce.2 = (f32[3,32]{1,0:T(4,128)S(1)}, f32[3]{0:T(128)S(1)}) all-reduce(f32[3,32]{1,0:T(4,128)S(1)} %bitcast.93, f32[3]{0:T(128)S(1)} %fusion.71), channel_id=1, replica_groups=mesh['dp'=8,'tensor'=4] {'tensor'}, use_global_device_ids=true, to_apply=%region_2.0 | all-reduce | flops 99 | bytes 792 | tf_op jit(solution)/shard_map/while/body/eval_jaxpr/psum | solution.py:15
  520.3 8.5 %all-reduce.2 = (f32[3,32]{1,0:T(4,128)S(1)}, f32[3]{0:T(128)S(1)}) all-reduce(f32[3,32]{1,0:T(4,128)S(1)} %bitcast.93, f32[3]{0:T(128)S(1)} %fusion.71), channel_id=1, replica_groups=mesh['dp'=8,'tensor'=4] {'tensor'}, use_global_device_ids=true, to_apply=%region_2.0 | all-reduce | flops 99 | bytes 792 | tf_op jit(solution)/shard_map/while/body/eval_jaxpr/psum | solution.py:15
  530.7 10.3 %all-reduce.2 = (f32[3,32]{1,0:T(4,128)S(1)}, f32[3]{0:T(128)S(1)}) all-reduce(f32[3,32]{1,0:T(4,128)S(1)} %bitcast.93, f32[3]{0:T(128)S(1)} %fusion.71), channel_id=1, replica_groups=mesh['dp'=8,'tensor'=4] {'tensor'}, use_global_device_ids=true, to_apply=%region_2.0 | all-reduce | flops 99 | bytes 792 | tf_op jit(solution)/shard_map/while/body/eval_jaxpr/psum | solution.py:15
  543.0 8.5 %all-reduce.2 = (f32[3,32]{1,0:T(4,128)S(1)}, f32[3]{0:T(128)S(1)}) all-reduce(f32[3,32]{1,0:T(4,128)S(1)} %bitcast.93, f32[3]{0:T(128)S(1)} %fusion.71), channel_id=1, replica_groups=mesh['dp'=8,'tensor'=4] {'tensor'}, use_global_device_ids=true, to_apply=%region_2.0 | all-reduce | flops 99 | bytes 792 | tf_op jit(solution)/shard_map/while/body/eval_jaxpr/psum | solution.py:15
  553.6 10.2 %all-reduce.2 = (f32[3,32]{1,0:T(4,128)S(1)}, f32[3]{0:T(128)S(1)}) all-reduce(f32[3,32]{1,0:T(4,128)S(1)} %bitcast.93, f32[3]{0:T(128)S(1)} %fusion.71), channel_id=1, replica_groups=mesh['dp'=8,'tensor'=4] {'tensor'}, use_global_device_ids=true, to_apply=%region_2.0 | all-reduce | flops 99 | bytes 792 | tf_op jit(solution)/shard_map/while/body/eval_jaxpr/psum | solution.py:15
  565.8 8.5 %all-reduce.2 = (f32[3,32]{1,0:T(4,128)S(1)}, f32[3]{0:T(128)S(1)}) all-reduce(f32[3,32]{1,0:T(4,128)S(1)} %bitcast.93, f32[3]{0:T(128)S(1)} %fusion.71), channel_id=1, replica_groups=mesh['dp'=8,'tensor'=4] {'tensor'}, use_global_device_ids=true, to_apply=%region_2.0 | all-reduce | flops 99 | bytes 792 | tf_op jit(solution)/shard_map/while/body/eval_jaxpr/psum | solution.py:15
  576.3 10.2 %all-reduce.2 = (f32[3,32]{1,0:T(4,128)S(1)}, f32[3]{0:T(128)S(1)}) all-reduce(f32[3,32]{1,0:T(4,128)S(1)} %bitcast.93, f32[3]{0:T(128)S(1)} %fusion.71), channel_id=1, replica_groups=mesh['dp'=8,'tensor'=4] {'tensor'}, use_global_device_ids=true, to_apply=%region_2.0 | all-reduce | flops 99 | bytes 792 | tf_op jit(solution)/shard_map/while/body/eval_jaxpr/psum | solution.py:15
  588.5 8.5 %all-reduce.2 = (f32[3,32]{1,0:T(4,128)S(1)}, f32[3]{0:T(128)S(1)}) all-reduce(f32[3,32]{1,0:T(4,128)S(1)} %bitcast.93, f32[3]{0:T(128)S(1)} %fusion.71), channel_id=1, replica_groups=mesh['dp'=8,'tensor'=4] {'tensor'}, use_global_device_ids=true, to_apply=%region_2.0 | all-reduce | flops 99 | bytes 792 | tf_op jit(solution)/shard_map/while/body/eval_jaxpr/psum | solution.py:15
  599.0 10.2 %all-reduce.2 = (f32[3,32]{1,0:T(4,128)S(1)}, f32[3]{0:T(128)S(1)}) all-reduce(f32[3,32]{1,0:T(4,128)S(1)} %bitcast.93, f32[3]{0:T(128)S(1)} %fusion.71), channel_id=1, replica_groups=mesh['dp'=8,'tensor'=4] {'tensor'}, use_global_device_ids=true, to_apply=%region_2.0 | all-reduce | flops 99 | bytes 792 | tf_op jit(solution)/shard_map/while/body/eval_jaxpr/psum | solution.py:15
  611.2 8.5 %all-reduce.2 = (f32[3,32]{1,0:T(4,128)S(1)}, f32[3]{0:T(128)S(1)}) all-reduce(f32[3,32]{1,0:T(4,128)S(1)} %bitcast.93, f32[3]{0:T(128)S(1)} %fusion.71), channel_id=1, replica_groups=mesh['dp'=8,'tensor'=4] {'tensor'}, use_global_device_ids=true, to_apply=%region_2.0 | all-reduce | flops 99 | bytes 792 | tf_op jit(solution)/shard_map/while/body/eval_jaxpr/psum | solution.py:15
  620.6 1.5 fusion.34
  623.1 1.1 fusion.11
  624.2 1.1 fusion.10
  625.4 1.1 fusion.9
  626.5 1.3 pad_maximum_fusion
  628.5 130.8 %all-reduce.8.cloned.1.call-done = f32[3,4096,32]{1,2,0:T(8,128)} async-done(((f32[3,4096,32]{1,2,0:T(8,128)}), f32[3,4096,32]{1,2,0:T(8,128)}) %all-reduce.8.cloned.1.call-update) | async-done | bytes 1572880 | tf_op jit(solution)/shard_map/psum | solution.py:67
  759.3 1.8 dynamic-slice_multiply_fusion
  (270 shorter events, 56.3 us)
Async XLA Ops:
  7.2 42.2 %all-gather.11.cloned.1.call-start = ((), (), s32[]{:S(2)}) async-start(), calls=%async_computation.3 | async-start | bytes 1966080 | tf_op jit(solution)/shard_map/all_gather | solution.py:46
  7.9 87.9 %all-gather.9.cloned.1.call-start = ((), (), s32[]{:S(2)}) async-start(), calls=%async_computation.2 | async-start | bytes 2621440 | tf_op jit(solution)/shard_map/all_gather | solution.py:29
  8.6 133.4 %all-gather.5.cloned.1.call-start = ((), (), s32[]{:S(2)}) async-start(), calls=%async_computation | async-start | bytes 2621440 | tf_op jit(solution)/shard_map/all_gather | solution.py:30
  9.4 184.5 %all-gather.7.cloned.1.call-start = ((), (), s32[]{:S(2)}) async-start(), calls=%async_computation.1 | async-start | bytes 8257536 | tf_op jit(solution)/shard_map/all_gather | solution.py:40
  10.0 245.0 %all-reduce.6.cloned.1.call-start = ((), (), s32[]{:S(2)}) async-start(), calls=%async_computation.4 | async-start | bytes 688128 | tf_op jit(solution)/shard_map/psum | solution.py:57
  95.8 3.7 copy-start
  193.9 7.2 copy-start.3
  200.4 2.0 copy-start.2
  202.2 557.2 %all-reduce.8.cloned.1.call-start = ((), (), s32[]{:S(2)}) async-start(), calls=%async_computation.5 | async-start | bytes 3145728 | tf_op jit(solution)/shard_map/psum | solution.py:67
  623.1 2.3 copy-start.1
Sparse Core Ops, SparseCore 0:
  9.6 39.7 all-gather.10
  51.0 44.7 all-gather.8
  97.4 44.6 all-gather.4
  143.8 50.0 all-gather.6
  202.3 52.6 all-reduce.5
  627.9 131.3 all-reduce.7
where the time goes:
time: 770 us; the launch traced here: 768 us
  waiting for transfers between devices  359 us (47%)
  blocking collectives  302 us (39%)
  matrix products  46.6 us (6%)
  local copies, waits for them, and re-layouts  30.5 us (4%)
  other arithmetic  15.1 us (2%)
  between operations  14.2 us (2%)
    psum x32, blocking collectives, column_turn(): correlation, square = lax.psum((correlation, square), 'tensor')  302 us
    psum x1, waiting for transfers between devices, shards(): right_full = lax.psum(right_local, ('dp', 'tensor')) / replicas_count  131 us
    psum x1, waiting for transfers between devices, shards(): left_raw = lax.psum(jnp.stack(lefts), 'dp')  52.6 us
    all_gather x1, waiting for transfers between devices, shards(): lax.all_gather(down_weight, 'dp', axis=1, tiled=True)  47.6 us
    all_gather x1, waiting for transfers between devices, shards(): lax.all_gather(inputs, 'tensor', axis=1, tiled=True)  46.4 us
    all_gather x1, waiting for transfers between devices, shards(): lax.all_gather(grad_out, 'tensor', axis=1, tiled=True)  39.6 us
    all_gather x1, waiting for transfers between devices, shards(): warm_full = lax.all_gather(warm_start, 'tensor', axis=1, tiled=True)  39.4 us
    dynamic_slice x32, local copies, waits for them, and re-layouts, column_turn(): column = lax.dynamic_slice_in_dim(block, column_index, 1, 2)[:, :, 0]  28.9 us
  transfers between devices with their start and end apart: 6, of which 6 were waited for; matrix products, arithmetic and copies ran while one was open for 2% of the time, Pallas kernels for 0%

commit v1 on v0

v1 whole, which is shorter than its diff:
```python
import functools

import jax
import jax.numpy as jnp
from jax import lax
from jax.experimental import pallas as pl
from jax.experimental.pallas import tpu as pltpu
from jax.sharding import PartitionSpec as P

F32 = jnp.float32
BF16 = jnp.bfloat16
MESH = pl.DeviceIdType.MESH
HIGH = lax.Precision.HIGHEST
NN = (((1,), (0,)), ((), ()))
NT = (((1,), (1,)), ((), ()))


def flipped(index, mask):
    result, bit = index, 0
    while (1 << bit) <= mask:
        if mask & (1 << bit):
            result = result + (1 << bit) * (1 - 2 * (lax.div(index, 1 << bit) % 2))
        bit += 1
    return result


def exact_dot(left, right, dims):
    rows = left.shape[0]
    first = left.astype(BF16)
    rest = left - first.astype(F32)
    second = rest.astype(BF16)
    third = (rest - second.astype(F32)).astype(BF16)
    out = lax.dot_general(
        jnp.concatenate([first, second, third], axis=0), right, dims, preferred_element_type=F32
    )
    return out[:rows] + (out[rows : 2 * rows] + out[2 * rows :])


def inverse_cholesky(gram):
    count, rank, _ = gram.shape
    row_id = lax.broadcasted_iota(jnp.int32, (count, rank, rank), 1)
    col_id = lax.broadcasted_iota(jnp.int32, (count, rank, rank), 2)
    work = jnp.concatenate([(row_id == col_id).astype(F32), gram], axis=2)
    row_wide = lax.broadcasted_iota(jnp.int32, work.shape, 1)
    scale = jnp.zeros((count, rank, 1), F32)
    row_thin = lax.broadcasted_iota(jnp.int32, scale.shape, 1)
    for step in range(rank):
        row = work[:, step : step + 1, :]
        pivot = work[:, step : step + 1, rank + step : rank + step + 1]
        scale = jnp.where(row_thin == step, lax.rsqrt(pivot), scale)
        if step < rank - 1:
            column = work[:, :, rank + step : rank + step + 1]
            factor = column / pivot
            work = work - jnp.where(row_wide > step, factor * row, 0.0)
    return work[:, :, :rank] * scale


class Exchange:
    def __init__(self, axis, count, refs):
        self.axis, self.count = axis, count
        self.part, self.come, self.full, self.sems = refs
        self.me = lax.axis_index(axis)
        self.sent = []

    def store(self, row, value):
        share = self.part.shape[1]
        done = 0
        while done < value.shape[0]:
            index, offset = (row + done) // share, (row + done) % share
            size = min(share - offset, value.shape[0] - done)
            self.part[index, offset : offset + size, :] = value[done : done + size]
            done += size

    def scatter(self):
        self.copies = []
        for step in range(1, self.count):
            peer = lax.rem(self.me + step, self.count)
            copy = pltpu.make_async_remote_copy(
                src_ref=self.part.at[peer],
                dst_ref=self.come.at[step - 1],
                send_sem=self.sems.at[0, step - 1],
                recv_sem=self.sems.at[1, step - 1],
                device_id={self.axis: peer},
                device_id_type=MESH,
            )
            copy.start()
            self.copies.append(copy)

    def gather(self):
        total = self.part[self.me]
        for step in range(1, self.count):
            self.copies[step - 1].wait_recv()
            total = total + self.come[step - 1]
        self.full[self.me] = total
        self.later = []
        for step in range(1, self.count):
            peer = lax.rem(self.me + step, self.count)
            copy = pltpu.make_async_remote_copy(
                src_ref=self.full.at[self.me],
                dst_ref=self.full.at[self.me],
                send_sem=self.sems.at[2, step - 1],
                recv_sem=self.sems.at[3, step - 1],
                device_id={self.axis: peer},
                device_id_type=MESH,
            )
            copy.start()
            self.later.append(copy)

    def wait(self):
        for step in range(1, self.count):
            source = lax.rem(self.me + self.count - step, self.count)
            pltpu.make_async_remote_copy(
                src_ref=self.full.at[source],
                dst_ref=self.full.at[source],
                send_sem=self.sems.at[2, step - 1],
                recv_sem=self.sems.at[3, step - 1],
                device_id={self.axis: lax.rem(self.me + step, self.count)},
                device_id_type=MESH,
            ).wait_recv()

    def load(self, row, size):
        share = self.full.shape[1]
        pieces, done = [], 0
        while done < size:
            index, offset = (row + done) // share, (row + done) % share
            take = min(share - offset, size - done)
            pieces.append(self.full[index, offset : offset + take, :])
            done += take
        return jnp.concatenate(pieces, axis=0)

    def finish(self):
        for copy in self.copies + self.later:
            copy.wait_send()


def kernel(n_dp, n_tp, x_ref, g_ref, gate_ref, up_ref, w_ref, warm_ref, left_out, right_out,
           wbuf, wsend, wrecv, gfull, gsend, grecv, hg, gate_grad, up_grad, hidden,
           p0, p1, p2, p3, l0, l1, l2, l3, m0, m1, m2, m3, r0, r1, r2, r3,
           gram_own, gram_come, gram_sems):
    d, z = lax.axis_index("dp"), lax.axis_index("tensor")
    tokens = x_ref.shape[0]
    rank = warm_ref.shape[1]
    weight_columns = w_ref.shape[1]
    per = n_dp // n_tp
    halves = wbuf.shape[1]
    width = weight_columns // halves
    bits = n_dp.bit_length() - 1

    barrier = pltpu.get_barrier_semaphore()
    for step in range(1, n_dp):
        pl.semaphore_signal(barrier, inc=1, device_id={"dp": lax.rem(d + step, n_dp)}, device_id_type=MESH)
    for step in range(1, n_tp):
        pl.semaphore_signal(barrier, inc=1, device_id={"tensor": lax.rem(z + step, n_tp)}, device_id_type=MESH)
    for part in range(per):
        gfull[z * per + part] = g_ref[:, part * weight_columns : (part + 1) * weight_columns]
    pl.semaphore_wait(barrier, n_dp - 1 + n_tp - 1)

    def shard(index):
        return gfull.at[pl.ds(index * per, per)]

    def line_copy(way, hop):
        source = z - hop if way == 0 else z + hop
        target = z + 1 if way == 0 else z - 1
        return pltpu.make_async_remote_copy(
            src_ref=shard(source), dst_ref=shard(source),
            send_sem=gsend.at[way, hop], recv_sem=grecv.at[way, hop],
            device_id={"tensor": target}, device_id_type=MESH,
        )

    def line_sends(way, hop):
        if way == 0:
            return jnp.logical_and(z - hop >= 0, z < n_tp - 1)
        return jnp.logical_and(z + hop <= n_tp - 1, z > 0)

    def line_start(hop):
        for way in (0, 1):
            @pl.when(line_sends(way, hop))
            def _():
                line_copy(way, hop).start()

    def line_wait(hop):
        for way in (0, 1):
            source = z - 1 - hop if way == 0 else z + 1 + hop
            @pl.when(source >= 0 if way == 0 else source <= n_tp - 1)
            def _():
                pltpu.make_async_remote_copy(
                    src_ref=shard(source), dst_ref=shard(source),
                    send_sem=gsend.at[way, hop], recv_sem=grecv.at[way, hop],
                    device_id={"tensor": z - 1 if way == 0 else z + 1}, device_id_type=MESH,
                ).wait_recv()

    orders = [list(range(1, bits)) + [0], list(range(bits - 1, 0, -1)) + [0]]
    weight_copies = {}

    def weight_source(slot, half):
        if slot == 0:
            return w_ref.at[:, pl.ds(half * width, width)]
        return wbuf.at[slot, half]

    def weight_send(slot, half, first):
        for bit in orders[half][first:]:
            target = slot ^ (1 << bit)
            copy = pltpu.make_async_remote_copy(
                src_ref=weight_source(slot, half), dst_ref=wbuf.at[target, half],
                send_sem=wsend.at[target, half], recv_sem=wrecv.at[target, half],
                device_id={"dp": flipped(d, 1 << bit)}, device_id_type=MESH,
            )
            copy.start()
            weight_copies[target, half] = copy

    def weight_wave(position):
        for index in range(1 << position):
            for half in range(halves):
                order = orders[half]
                slot = 1 << order[position]
                for place in range(position):
                    if index & (1 << place):
                        slot |= 1 << order[place]
                weight_copies[slot, half].wait_recv()
                weight_send(slot, half, position + 1)

    line_start(0)
    for half in range(halves):
        weight_send(0, half, 0)

    total_p = Exchange("tensor", n_tp, (p0, p1, p2, p3))
    total_l = Exchange("dp", n_dp, (l0, l1, l2, l3))
    total_m = Exchange("tensor", n_tp, (m0, m1, m2, m3))
    total_r = Exchange("dp", n_dp, (r0, r1, r2, r3))
    rights = (x_ref, x_ref, g_ref)
    lefts = (gate_grad, up_grad, hidden)
    for k in range(3):
        total_p.store(k * rank, exact_dot(warm_ref[k], rights[k][...], NT))
    total_p.scatter()

    gate = gate_ref[...].astype(F32)
    up = up_ref[...].astype(F32)
    sigma = 1.0 / (1.0 + jnp.exp(-gate))
    hidden[...] = (gate * sigma * up).astype(BF16)

    total_p.gather()
    total_p.wait()
    for hop in range(n_tp - 2):
        line_wait(hop)
        line_start(hop + 1)
        if hop < bits - 1:
            weight_wave(hop)
    for position in range(n_tp - 2, bits - 1):
        weight_wave(position)
    line_wait(n_tp - 2)

    hg[...] = jnp.zeros_like(hg)

    def use(slot, half):
        hg[...] += lax.dot_general(
            gfull[flipped(d, slot), :, half * width : (half + 1) * width],
            weight_source(slot, half)[...], NT, preferred_element_type=F32,
        )

    for slot in range(0, n_dp, 2):
        for half in range(halves):
            use(slot, half)
    for slot in range(1, n_dp, 2):
        for half in range(halves):
            weight_copies[slot, half].wait_recv()
            use(slot, half)

    gate = gate_ref[...].astype(F32)
    up = up_ref[...].astype(F32)
    sigma = 1.0 / (1.0 + jnp.exp(-gate))
    hidden_grad = hg[...]
    gate_grad[...] = (hidden_grad * up * sigma * (1.0 + gate * (1.0 - sigma))).astype(BF16)
    up_grad[...] = (hidden_grad * gate * sigma).astype(BF16)

    for k in range(3):
        total_l.store(k * rank, exact_dot(total_p.load(k * rank, rank), lefts[k][...], NN) * (1.0 / tokens))
    total_l.scatter()
    total_l.gather()
    total_l.wait()

    for k in range(3):
        raw = total_l.load(k * rank, rank)
        total_m.store(k * rank, exact_dot(raw, lefts[k][...], NT))
        gram_own[k] = lax.dot_general(raw, raw, NT, precision=HIGH, preferred_element_type=F32)
    total_m.scatter()
    gram_copies = []
    for step in range(1, n_tp):
        copy = pltpu.make_async_remote_copy(
            src_ref=gram_own, dst_ref=gram_come.at[step - 1],
            send_sem=gram_sems.at[0, step - 1], recv_sem=gram_sems.at[1, step - 1],
            device_id={"tensor": lax.rem(z + step, n_tp)}, device_id_type=MESH,
        )
        copy.start()
        gram_copies.append(copy)
    total_m.gather()
    total_m.wait()

    for k in range(3):
        total_r.store(k * rank, exact_dot(total_m.load(k * rank, rank), rights[k][...], NN))
    total_r.scatter()

    gram = gram_own[...]
    for step in range(1, n_tp):
        gram_copies[step - 1].wait_recv()
        gram = gram + gram_come[step - 1]
    inverse = inverse_cholesky(gram)
    for k in range(3):
        left_out[k] = lax.dot_general(
            inverse[k], total_l.load(k * rank, rank), NN, precision=HIGH, preferred_element_type=F32
        )

    total_r.gather()
    total_r.wait()
    for k in range(3):
        right_out[k] = lax.dot_general(
            inverse[k], total_r.load(k * rank, rank), NN, precision=HIGH, preferred_element_type=F32
        ) * (1.0 / (tokens * n_dp))

    for exchange in (total_p, total_l, total_m, total_r):
        exchange.finish()
    for copy in gram_copies + list(weight_copies.values()):
        copy.wait_send()
    for hop in range(n_tp - 1):
        for way in (0, 1):
            @pl.when(line_sends(way, hop))
            def _():
                line_copy(way, hop).wait_send()


def exchange_scratch(count, rows, width):
    share = rows // count
    return [
        pltpu.VMEM((count, share, width), F32),
        pltpu.VMEM((count - 1, share, width), F32),
        pltpu.VMEM((count, share, width), F32),
        pltpu.SemaphoreType.DMA((4, count - 1)),
    ]


def shards(n_dp, n_tp, inputs, grad_out, gate_pre, up_pre, down_weight, warm_start):
    tokens, own = inputs.shape
    hidden_units, weight_columns = down_weight.shape
    count, _, rank = warm_start.shape
    halves = 2 if weight_columns % 256 == 0 else 1
    vmem = pl.BlockSpec(memory_space=pltpu.VMEM)
    left, right = pl.pallas_call(
        functools.partial(kernel, n_dp, n_tp),
        out_shape=(
            jax.ShapeDtypeStruct((count, rank, hidden_units), F32),
            jax.ShapeDtypeStruct((count, rank, own), F32),
        ),
        in_specs=[vmem] * 6,
        out_specs=(vmem, vmem),
        scratch_shapes=[
            pltpu.VMEM((n_dp, halves, hidden_units, weight_columns // halves), BF16),
            pltpu.SemaphoreType.DMA((n_dp, halves)),
            pltpu.SemaphoreType.DMA((n_dp, halves)),
            pltpu.VMEM((n_dp, tokens, weight_columns), BF16),
            pltpu.SemaphoreType.DMA((2, n_tp - 1)),
            pltpu.SemaphoreType.DMA((2, n_tp - 1)),
            pltpu.VMEM((tokens, hidden_units), F32),
            pltpu.VMEM((tokens, hidden_units), BF16),
            pltpu.VMEM((tokens, hidden_units), BF16),
            pltpu.VMEM((tokens, hidden_units), BF16),
            *exchange_scratch(n_tp, count * rank, tokens),
            *exchange_scratch(n_dp, count * rank, hidden_units),
            *exchange_scratch(n_tp, count * rank, tokens),
            *exchange_scratch(n_dp, count * rank, own),
            pltpu.VMEM((count, rank, rank), F32),
            pltpu.VMEM((n_tp - 1, count, rank, rank), F32),
            pltpu.SemaphoreType.DMA((2, n_tp - 1)),
        ],
        compiler_params=pltpu.CompilerParams(
            collective_id=0, has_side_effects=True, vmem_limit_bytes=48 * 1024 * 1024
        ),
        name="powersgd",
    )(inputs, grad_out, gate_pre, up_pre, down_weight, jnp.swapaxes(warm_start, 1, 2))
    return jnp.swapaxes(left, 1, 2), jnp.swapaxes(right, 1, 2)


def solution(mesh):
    placed = (
        P("dp", "tensor"),
        P("dp", "tensor"),
        P("dp", "tensor"),
        P("dp", "tensor"),
        P("tensor", "dp"),
        P(None, "tensor", None),
    )
    return jax.shard_map(
        functools.partial(shards, mesh.shape["dp"], mesh.shape["tensor"]),
        mesh=mesh,
        in_specs=placed,
        out_specs=(P(None, "tensor", None), P(None, "tensor", None)),
        check_vma=False,
    )
```

time: 770 us -> 99.5 us (0.13)
  waiting for transfers between devices: 359 us -> 0 us
  blocking collectives: 302 us -> 0 us
  Pallas kernels: 0 us -> 90.1 us
  matrix products: 46.6 us -> 0 us
  local copies, waits for them, and re-layouts: 30.5 us -> 7.76 us
  other arithmetic: 15.1 us -> 0 us
  between operations: 14.2 us -> 0.65 us
    psum x32 -> x0, blocking collectives: 302 us -> none  [column_turn(): correlation, square = lax.psum((correlation, square), 'tensor')]
    psum x2 -> x0, waiting for transfers between devices: 183 us -> none  [the longest x1 131 us: shards(): right_full = lax.psum(right_local, ('dp', 'tensor')) / replicas_count]
    all_gather x4 -> x0, waiting for transfers between devices: 173 us -> none  [the longest x1 47.6 us: shards(): lax.all_gather(down_weight, 'dp', axis=1, tiled=True)]
    pallas_call x0 -> x1, Pallas kernels: none -> 90.1 us  [shards(): pl.pallas_call(functools.partial(kernel, n_dp, n_tp), out_shape=(jax.Shap...]
    dot_general x77 -> x0, matrix products: 46.6 us -> none  [the longest x32 12.3 us: column_turn(): correlation = jnp.einsum('kfr,kf->kr', basis, column, precision=high)]
    dynamic_slice x32 -> x0, local copies, waits for them, and re-layouts: 28.9 us -> none  [column_turn(): column = lax.dynamic_slice_in_dim(block, column_index, 1, 2)[:, :, 0]]
    reduce_sum x64 -> x0, other arithmetic: 8.31 us -> none  [the longest x32 4.54 us: column_turn(): square = jnp.sum(column * column, axis=1)]
  transfers between devices with their start and end apart: 6 -> 0, of which waited for: 6 -> 0; matrix products, arithmetic and copies ran while one was open for 2% -> 0% of each run, Pallas kernels for 0% -> 0%
where the time goes in v1:
time: 99.5 us; the launch traced here: 98.5 us
  Pallas kernels  90.1 us (91%)
  local copies, waits for them, and re-layouts  7.76 us (8%)
    pallas_call x1, Pallas kernels, shards(): pl.pallas_call(functools.partial(kernel, n_dp, n_tp), out_shape=(jax.Shap...  90.1 us
    unnamed x14, local copies, waits for them, and re-layouts  7.76 us

profile of v1, /device:TPU:0, one launch (start us, length us, event | category | flops | bytes accessed | tf_op | source)
XLA Modules:
  0.0 98.5 jit_solution(5446158996126729800)
XLA Ops:
  0.6 0.0 copy-start
  0.6 1.2 %copy-done = bf16[896,512]{1,0:T(8,128)(2,1)S(1)} copy-done((bf16[896,512]{1,0:T(8,128)(2,1)S(1)}, bf16[896,512]{1,0:T(8,128)(2,1)}, u32[]{:S(2)}) %copy-start) | copy-done | bytes 917528
  1.8 0.0 copy-start.1
  1.8 1.0 %copy-done.1 = bf16[256,1024]{1,0:T(8,128)(2,1)S(1)} copy-done((bf16[256,1024]{1,0:T(8,128)(2,1)S(1)}, bf16[256,1024]{1,0:T(8,128)(2,1)}, u32[]{:S(2)}) %copy-start.1) | copy-done | bytes 524312
  2.9 0.0 copy-start.2
  2.9 1.0 %copy-done.2 = bf16[256,1024]{1,0:T(8,128)(2,1)S(1)} copy-done((bf16[256,1024]{1,0:T(8,128)(2,1)S(1)}, bf16[256,1024]{1,0:T(8,128)(2,1)}, u32[]{:S(2)}) %copy-start.2) | copy-done | bytes 524312
  3.9 0.0 copy-start.3
  3.9 1.0 %copy-done.3 = bf16[256,896]{1,0:T(8,128)(2,1)S(1)} copy-done((bf16[256,896]{1,0:T(8,128)(2,1)S(1)}, bf16[256,896]{1,0:T(8,128)(2,1)}, u32[]{:S(2)}) %copy-start.3) | copy-done | bytes 458776
  4.9 0.0 copy-start.4
  4.9 1.0 %copy-done.4 = bf16[256,896]{1,0:T(8,128)(2,1)S(1)} copy-done((bf16[256,896]{1,0:T(8,128)(2,1)S(1)}, bf16[256,896]{1,0:T(8,128)(2,1)}, u32[]{:S(2)}) %copy-start.4) | copy-done | bytes 458776
  5.9 0.0 copy-start.5
  5.9 1.0 %copy-done.5 = f32[3,1024,32]{1,2,0:T(8,128)S(1)} copy-done((f32[3,1024,32]{1,2,0:T(8,128)S(1)}, f32[3,1024,32]{1,2,0:T(8,128)}, u32[]{:S(2)}) %copy-start.5) | copy-done | bytes 393240
  6.9 90.1 %powersgd.1 = (f32[3,32,896]{2,1,0:T(8,128)S(1)}, f32[3,32,1024]{2,1,0:T(8,128)S(1)}) custom-call(bf16[256,1024]{1,0:T(8,128)(2,1)S(1)} %copy-done.1, bf16[256,1024]{1,0:T(8,128)(2,1)S(1)} %copy-done.2, bf16[256,896]{1,0:T(8,128)(2,1)S(1)} %copy-done.3, bf16[256,896]{1,0:T(8,128)(2,1)S(1)} %copy-done.4, bf16[896,512]{1,0:T(8,128)(2,1)S(1)} %copy-done, ...), custom_call_target="tpu_custom_call" | custom-call | tf_op jit(solution)/shard_map/powersgd/pallas_call | solution.py:346
  97.0 0.7 copy.10
  97.7 0.7 copy.11
Async XLA Ops:
  0.6 1.2 %copy-start = (bf16[896,512]{1,0:T(8,128)(2,1)S(1)}, bf16[896,512]{1,0:T(8,128)(2,1)}, u32[]{:S(2)}) copy-start(bf16[896,512]{1,0:T(8,128)(2,1)} %w_ref.1) | copy-start | bytes 2752516
  1.8 1.0 %copy-start.1 = (bf16[256,1024]{1,0:T(8,128)(2,1)S(1)}, bf16[256,1024]{1,0:T(8,128)(2,1)}, u32[]{:S(2)}) copy-start(bf16[256,1024]{1,0:T(8,128)(2,1)} %x_ref.1) | copy-start | bytes 1572868
  2.9 1.0 %copy-start.2 = (bf16[256,1024]{1,0:T(8,128)(2,1)S(1)}, bf16[256,1024]{1,0:T(8,128)(2,1)}, u32[]{:S(2)}) copy-start(bf16[256,1024]{1,0:T(8,128)(2,1)} %g_ref.1) | copy-start | bytes 1572868
  3.9 1.0 %copy-start.3 = (bf16[256,896]{1,0:T(8,128)(2,1)S(1)}, bf16[256,896]{1,0:T(8,128)(2,1)}, u32[]{:S(2)}) copy-start(bf16[256,896]{1,0:T(8,128)(2,1)} %gate_ref.1) | copy-start | bytes 1376260
  4.9 1.0 %copy-start.4 = (bf16[256,896]{1,0:T(8,128)(2,1)S(1)}, bf16[256,896]{1,0:T(8,128)(2,1)}, u32[]{:S(2)}) copy-start(bf16[256,896]{1,0:T(8,128)(2,1)} %up_ref.1) | copy-start | bytes 1376260
  5.9 1.0 %copy-start.5 = (f32[3,1024,32]{1,2,0:T(8,128)S(1)}, f32[3,1024,32]{1,2,0:T(8,128)}, u32[]{:S(2)}) copy-start(f32[3,1024,32]{1,2,0:T(8,128)} %param.11) | copy-start | bytes 1179652

commit v2 on v1

--- a/solution.py
+++ b/solution.py
@@ -60,7 +60,7 @@
         self.axis, self.count = axis, count
         self.part, self.come, self.full, self.sems = refs
         self.me = lax.axis_index(axis)
-        self.sent = []
+        self.copies, self.later = [], []
 
     def store(self, row, value):
         share = self.part.shape[1]
@@ -72,7 +72,6 @@
             done += size
 
     def scatter(self):
-        self.copies = []
         for step in range(1, self.count):
             peer = lax.rem(self.me + step, self.count)
             copy = pltpu.make_async_remote_copy(
@@ -92,7 +91,6 @@
             self.copies[step - 1].wait_recv()
             total = total + self.come[step - 1]
         self.full[self.me] = total
-        self.later = []
         for step in range(1, self.count):
             peer = lax.rem(self.me + step, self.count)
             copy = pltpu.make_async_remote_copy(
@@ -133,14 +131,14 @@
             copy.wait_send()
 
 
-def kernel(n_dp, n_tp, x_ref, g_ref, gate_ref, up_ref, w_ref, warm_ref, left_out, right_out,
-           wbuf, wsend, wrecv, gfull, gsend, grecv, hg, gate_grad, up_grad, hidden,
+def kernel(n_dp, n_tp, x_hbm, g_hbm, gate_hbm, up_hbm, w_hbm, warm_hbm, left_out, right_out,
+           x_ref, gate_ref, up_ref, warm_ref, load_sems, wbuf, wsend, wrecv, gfull, gsend, grecv, hg, gate_grad, up_grad, hidden,
            p0, p1, p2, p3, l0, l1, l2, l3, m0, m1, m2, m3, r0, r1, r2, r3,
            gram_own, gram_come, gram_sems):
     d, z = lax.axis_index("dp"), lax.axis_index("tensor")
     tokens = x_ref.shape[0]
     rank = warm_ref.shape[1]
-    weight_columns = w_ref.shape[1]
+    weight_columns = w_hbm.shape[1]
     per = n_dp // n_tp
     halves = wbuf.shape[1]
     width = weight_columns // halves
@@ -151,8 +149,26 @@
         pl.semaphore_signal(barrier, inc=1, device_id={"dp": lax.rem(d + step, n_dp)}, device_id_type=MESH)
     for step in range(1, n_tp):
         pl.semaphore_signal(barrier, inc=1, device_id={"tensor": lax.rem(z + step, n_tp)}, device_id_type=MESH)
-    for part in range(per):
-        gfull[z * per + part] = g_ref[:, part * weight_columns : (part + 1) * weight_columns]
+
+    loads = []
+
+    def load(source, target):
+        copy = pltpu.make_async_copy(source, target, load_sems.at[len(loads)])
+        copy.start()
+        loads.append(copy)
+        return copy
+
+    load_g = [
+        load(g_hbm.at[:, pl.ds(part * weight_columns, weight_columns)], gfull.at[z * per + part])
+        for part in range(per)
+    ]
+    load_w = [
+        load(w_hbm.at[:, pl.ds(half * width, width)], wbuf.at[0, half]) for half in range(halves)
+    ]
+    load_warm, load_x = load(warm_hbm, warm_ref), load(x_hbm, x_ref)
+    load_gate, load_up = load(gate_hbm, gate_ref), load(up_hbm, up_ref)
+    for copy in load_g:
+        copy.wait()
     pl.semaphore_wait(barrier, n_dp - 1 + n_tp - 1)
 
     def shard(index):
@@ -192,16 +208,11 @@
     orders = [list(range(1, bits)) + [0], list(range(bits - 1, 0, -1)) + [0]]
     weight_copies = {}
 
-    def weight_source(slot, half):
-        if slot == 0:
-            return w_ref.at[:, pl.ds(half * width, width)]
-        return wbuf.at[slot, half]
-
     def weight_send(slot, half, first):
         for bit in orders[half][first:]:
             target = slot ^ (1 << bit)
             copy = pltpu.make_async_remote_copy(
-                src_ref=weight_source(slot, half), dst_ref=wbuf.at[target, half],
+                src_ref=wbuf.at[slot, half], dst_ref=wbuf.at[target, half],
                 send_sem=wsend.at[target, half], recv_sem=wrecv.at[target, half],
                 device_id={"dp": flipped(d, 1 << bit)}, device_id_type=MESH,
             )
@@ -219,20 +230,43 @@
                 weight_copies[slot, half].wait_recv()
                 weight_send(slot, half, position + 1)
 
+    gram_copies = []
+
+    def finish():
+        for exchange in (total_p, total_l, total_m, total_r):
+            exchange.finish()
+        for copy in gram_copies + list(weight_copies.values()):
+            copy.wait_send()
+        for hop in range(n_tp - 1):
+            for way in (0, 1):
+                @pl.when(line_sends(way, hop))
+                def _():
+                    line_copy(way, hop).wait_send()
+
     line_start(0)
     for half in range(halves):
+        load_w[half].wait()
         weight_send(0, half, 0)
 
     total_p = Exchange("tensor", n_tp, (p0, p1, p2, p3))
     total_l = Exchange("dp", n_dp, (l0, l1, l2, l3))
     total_m = Exchange("tensor", n_tp, (m0, m1, m2, m3))
     total_r = Exchange("dp", n_dp, (r0, r1, r2, r3))
-    rights = (x_ref, x_ref, g_ref)
     lefts = (gate_grad, up_grad, hidden)
-    for k in range(3):
-        total_p.store(k * rank, exact_dot(warm_ref[k], rights[k][...], NT))
+
+    def right(k):
+        if k < 2:
+            return x_ref[...]
+        return jnp.concatenate([gfull[z * per + part] for part in range(per)], axis=1)
+
+    load_warm.wait()
+    load_x.wait()
+    for k in range(3):
+        total_p.store(k * rank, exact_dot(warm_ref[k], right(k), NT))
     total_p.scatter()
 
+    load_gate.wait()
+    load_up.wait()
     gate = gate_ref[...].astype(F32)
     up = up_ref[...].astype(F32)
     sigma = 1.0 / (1.0 + jnp.exp(-gate))
@@ -254,7 +288,7 @@
     def use(slot, half):
         hg[...] += lax.dot_general(
             gfull[flipped(d, slot), :, half * width : (half + 1) * width],
-            weight_source(slot, half)[...], NT, preferred_element_type=F32,
+            wbuf[slot, half], NT, preferred_element_type=F32,
         )
 
     for slot in range(0, n_dp, 2):
@@ -283,7 +317,6 @@
         total_m.store(k * rank, exact_dot(raw, lefts[k][...], NT))
         gram_own[k] = lax.dot_general(raw, raw, NT, precision=HIGH, preferred_element_type=F32)
     total_m.scatter()
-    gram_copies = []
     for step in range(1, n_tp):
         copy = pltpu.make_async_remote_copy(
             src_ref=gram_own, dst_ref=gram_come.at[step - 1],
@@ -296,7 +329,7 @@
     total_m.wait()
 
     for k in range(3):
-        total_r.store(k * rank, exact_dot(total_m.load(k * rank, rank), rights[k][...], NN))
+        total_r.store(k * rank, exact_dot(total_m.load(k * rank, rank), right(k), NN))
     total_r.scatter()
 
     gram = gram_own[...]
@@ -316,15 +349,7 @@
             inverse[k], total_r.load(k * rank, rank), NN, precision=HIGH, preferred_element_type=F32
         ) * (1.0 / (tokens * n_dp))
 
-    for exchange in (total_p, total_l, total_m, total_r):
-        exchange.finish()
-    for copy in gram_copies + list(weight_copies.values()):
-        copy.wait_send()
-    for hop in range(n_tp - 1):
-        for way in (0, 1):
-            @pl.when(line_sends(way, hop))
-            def _():
-                line_copy(way, hop).wait_send()
+    finish()
 
 
 def exchange_scratch(count, rows, width):
@@ -343,15 +368,21 @@
     count, _, rank = warm_start.shape
     halves = 2 if weight_columns % 256 == 0 else 1
     vmem = pl.BlockSpec(memory_space=pltpu.VMEM)
+    loads = 4 + halves + n_dp // n_tp
     left, right = pl.pallas_call(
         functools.partial(kernel, n_dp, n_tp),
         out_shape=(
             jax.ShapeDtypeStruct((count, rank, hidden_units), F32),
             jax.ShapeDtypeStruct((count, rank, own), F32),
         ),
-        in_specs=[vmem] * 6,
+        in_specs=[pl.BlockSpec(memory_space=pl.ANY)] * 6,
         out_specs=(vmem, vmem),
         scratch_shapes=[
+            pltpu.VMEM(inputs.shape, BF16),
+            pltpu.VMEM(gate_pre.shape, BF16),
+            pltpu.VMEM(up_pre.shape, BF16),
+            pltpu.VMEM((count, rank, own), F32),
+            pltpu.SemaphoreType.DMA((loads,)),
             pltpu.VMEM((n_dp, halves, hidden_units, weight_columns // halves), BF16),
             pltpu.SemaphoreType.DMA((n_dp, halves)),
             pltpu.SemaphoreType.DMA((n_dp, halves)),
@@ -371,7 +402,7 @@
             pltpu.SemaphoreType.DMA((2, n_tp - 1)),
         ],
         compiler_params=pltpu.CompilerParams(
-            collective_id=0, has_side_effects=True, vmem_limit_bytes=48 * 1024 * 1024
+            collective_id=0, has_side_effects=True, vmem_limit_bytes=56 * 1024 * 1024
         ),
         name="powersgd",
     )(inputs, grad_out, gate_pre, up_pre, down_weight, jnp.swapaxes(warm_start, 1, 2))

time: 99.5 us -> 94.9 us (0.954)
  local copies, waits for them, and re-layouts: 7.76 us -> 2.53 us
    unnamed x14 -> x4, local copies, waits for them, and re-layouts: 7.76 us -> 2.53 us
where the time goes in v2:
time: 94.9 us; the launch traced here: 94.2 us
  Pallas kernels  91 us (96%)
  local copies, waits for them, and re-layouts  2.53 us (3%)
    pallas_call x1, Pallas kernels, shards(): pl.pallas_call(functools.partial(kernel, n_dp, n_tp), out_shape=(jax.Shap...  91 us
    unnamed x4, local copies, waits for them, and re-layouts  2.53 us

profile of v2, /device:TPU:0, one launch (start us, length us, event | category | flops | bytes accessed | tf_op | source)
XLA Modules:
  0.0 94.2 jit_solution(13215317040223540329)
XLA Ops:
  0.6 91.0 %powersgd.1 = (f32[3,32,896]{2,1,0:T(8,128)}, f32[3,32,1024]{2,1,0:T(8,128)}) custom-call(bf16[256,1024]{1,0:T(8,128)(2,1)} %x_hbm.1, bf16[256,1024]{1,0:T(8,128)(2,1)} %g_hbm.1, bf16[256,896]{1,0:T(8,128)(2,1)} %gate_hbm.1, bf16[256,896]{1,0:T(8,128)(2,1)} %up_hbm.1, bf16[896,512]{1,0:T(8,128)(2,1)} %w_hbm.1, f32[3,32,1024]{2,1,0:T(8,128)} %bitcast.3), custom_call_target="tpu_custom_call" | custom-call | tf_op jit(solution)/shard_map/powersgd/pallas_call | solution.py:372
  91.7 0.0 copy-start
  91.7 1.8 %copy.10 = f32[3,896,32]{1,2,0:T(8,128)} copy(f32[3,896,32]{1,2,0:T(8,128)} %bitcast.5) | data formatting | bytes 688128
  93.5 0.0 copy-done
  93.5 0.7 copy.11
Async XLA Ops:
  91.7 1.8 %copy-start = (f32[3,32,1024]{2,1,0:T(8,128)S(1)}, f32[3,32,1024]{2,1,0:T(8,128)}, u32[]{:S(2)}) copy-start(f32[3,32,1024]{2,1,0:T(8,128)} %get-tuple-element.5) | copy-start | bytes 1179652

commit v3 on v2

--- a/solution.py
+++ b/solution.py
@@ -132,7 +132,7 @@
 
 
 def kernel(n_dp, n_tp, x_hbm, g_hbm, gate_hbm, up_hbm, w_hbm, warm_hbm, left_out, right_out,
-           x_ref, gate_ref, up_ref, warm_ref, load_sems, wbuf, wsend, wrecv, gfull, gsend, grecv, hg, gate_grad, up_grad, hidden,
+           x_ref, gate_ref, up_ref, warm_ref, load_sems, wbuf, wsend, wrecv, gfull, gsend, grecv, hg, gate_slope, up_slope, gate_grad, up_grad, hidden,
            p0, p1, p2, p3, l0, l1, l2, l3, m0, m1, m2, m3, r0, r1, r2, r3,
            gram_own, gram_come, gram_sems):
     d, z = lax.axis_index("dp"), lax.axis_index("tensor")
@@ -140,7 +140,7 @@
     rank = warm_ref.shape[1]
     weight_columns = w_hbm.shape[1]
     per = n_dp // n_tp
-    halves = wbuf.shape[1]
+    halves = wsend.shape[1]
     width = weight_columns // halves
     bits = n_dp.bit_length() - 1
 
@@ -163,7 +163,8 @@
         for part in range(per)
     ]
     load_w = [
-        load(w_hbm.at[:, pl.ds(half * width, width)], wbuf.at[0, half]) for half in range(halves)
+        load(w_hbm.at[:, pl.ds(half * width, width)], wbuf.at[d, :, pl.ds(half * width, width)])
+        for half in range(halves)
     ]
     load_warm, load_x = load(warm_hbm, warm_ref), load(x_hbm, x_ref)
     load_gate, load_up = load(gate_hbm, gate_ref), load(up_hbm, up_ref)
@@ -206,18 +207,21 @@
                 ).wait_recv()
 
     orders = [list(range(1, bits)) + [0], list(range(bits - 1, 0, -1)) + [0]]
-    weight_copies = {}
+    weight_copies = []
+
+    def weight_copy(slot, half, partner, sem_slot):
+        place = wbuf.at[flipped(d, slot), :, pl.ds(half * width, width)]
+        return pltpu.make_async_remote_copy(
+            src_ref=place, dst_ref=place,
+            send_sem=wsend.at[sem_slot, half], recv_sem=wrecv.at[sem_slot, half],
+            device_id={"dp": flipped(d, partner)}, device_id_type=MESH,
+        )
 
     def weight_send(slot, half, first):
         for bit in orders[half][first:]:
-            target = slot ^ (1 << bit)
-            copy = pltpu.make_async_remote_copy(
-                src_ref=wbuf.at[slot, half], dst_ref=wbuf.at[target, half],
-                send_sem=wsend.at[target, half], recv_sem=wrecv.at[target, half],
-                device_id={"dp": flipped(d, 1 << bit)}, device_id_type=MESH,
-            )
+            copy = weight_copy(slot, half, 1 << bit, slot ^ (1 << bit))
             copy.start()
-            weight_copies[target, half] = copy
+            weight_copies.append(copy)
 
     def weight_wave(position):
         for index in range(1 << position):
@@ -227,7 +231,7 @@
                 for place in range(position):
                     if index & (1 << place):
                         slot |= 1 << order[place]
-                weight_copies[slot, half].wait_recv()
+                weight_copy(slot, half, 1 << order[position], slot).wait_recv()
                 weight_send(slot, half, position + 1)
 
     gram_copies = []
@@ -235,7 +239,7 @@
     def finish():
         for exchange in (total_p, total_l, total_m, total_r):
             exchange.finish()
-        for copy in gram_copies + list(weight_copies.values()):
+        for copy in gram_copies + weight_copies:
             copy.wait_send()
         for hop in range(n_tp - 1):
             for way in (0, 1):
@@ -271,40 +275,46 @@
     up = up_ref[...].astype(F32)
     sigma = 1.0 / (1.0 + jnp.exp(-gate))
     hidden[...] = (gate * sigma * up).astype(BF16)
-
-    total_p.gather()
-    total_p.wait()
-    for hop in range(n_tp - 2):
+    gate_slope[...] = up * sigma * (1.0 + gate * (1.0 - sigma))
+    up_slope[...] = gate * sigma
+
+    def product(source):
+        total = None
+        for part in range(per):
+            block = source * per + part
+            term = lax.dot_general(gfull[block], wbuf[block], NT, preferred_element_type=F32)
+            total = term if total is None else total + term
+        return total
+
+    def line_use(hop):
+        for way in (0, 1):
+            source = z - 1 - hop if way == 0 else z + 1 + hop
+            @pl.when(source >= 0 if way == 0 else source <= n_tp - 1)
+            def _():
+                hg[...] += product(source)
+
+    last = n_tp - 2
+    waves = list(range(bits - 1))
+    for hop in range(last):
         line_wait(hop)
         line_start(hop + 1)
-        if hop < bits - 1:
-            weight_wave(hop)
-    for position in range(n_tp - 2, bits - 1):
+        if waves:
+            weight_wave(waves.pop(0))
+        if hop == 0:
+            total_p.gather()
+    for position in waves:
         weight_wave(position)
-    line_wait(n_tp - 2)
-
-    hg[...] = jnp.zeros_like(hg)
-
-    def use(slot, half):
-        hg[...] += lax.dot_general(
-            gfull[flipped(d, slot), :, half * width : (half + 1) * width],
-            wbuf[slot, half], NT, preferred_element_type=F32,
-        )
-
-    for slot in range(0, n_dp, 2):
-        for half in range(halves):
-            use(slot, half)
-    for slot in range(1, n_dp, 2):
-        for half in range(halves):
-            weight_copies[slot, half].wait_recv()
-            use(slot, half)
-
-    gate = gate_ref[...].astype(F32)
-    up = up_ref[...].astype(F32)
-    sigma = 1.0 / (1.0 + jnp.exp(-gate))
+    total_p.wait()
+    weight_wave(bits - 1)
+    hg[...] = product(z)
+    for hop in range(last):
+        line_use(hop)
+    line_wait(last)
+    line_use(last)
+
     hidden_grad = hg[...]
-    gate_grad[...] = (hidden_grad * up * sigma * (1.0 + gate * (1.0 - sigma))).astype(BF16)
-    up_grad[...] = (hidden_grad * gate * sigma).astype(BF16)
+    gate_grad[...] = (hidden_grad * gate_slope[...]).astype(BF16)
+    up_grad[...] = (hidden_grad * up_slope[...]).astype(BF16)
 
     for k in range(3):
         total_l.store(k * rank, exact_dot(total_p.load(k * rank, rank), lefts[k][...], NN) * (1.0 / tokens))
@@ -312,10 +322,11 @@
     total_l.gather()
     total_l.wait()
 
+    gram_own[...] = jnp.zeros_like(gram_own)
     for k in range(3):
         raw = total_l.load(k * rank, rank)
         total_m.store(k * rank, exact_dot(raw, lefts[k][...], NT))
-        gram_own[k] = lax.dot_general(raw, raw, NT, precision=HIGH, preferred_element_type=F32)
+        gram_own[:, k * rank : (k + 1) * rank] = lax.dot_general(raw, raw, NT, precision=HIGH, preferred_element_type=F32)
     total_m.scatter()
     for step in range(1, n_tp):
         copy = pltpu.make_async_remote_copy(
@@ -332,17 +343,19 @@
         total_r.store(k * rank, exact_dot(total_m.load(k * rank, rank), right(k), NN))
     total_r.scatter()
 
-    gram = gram_own[...]
+    gram = gram_own[:, : 3 * rank]
     for step in range(1, n_tp):
         gram_copies[step - 1].wait_recv()
-        gram = gram + gram_come[step - 1]
-    inverse = inverse_cholesky(gram)
+        gram = gram + gram_come[step - 1, :, : 3 * rank]
+    inverse = inverse_cholesky(
+        jnp.stack([gram[:, k * rank : (k + 1) * rank] for k in range(3)])
+    )
+    total_r.gather()
     for k in range(3):
         left_out[k] = lax.dot_general(
             inverse[k], total_l.load(k * rank, rank), NN, precision=HIGH, preferred_element_type=F32
         )
 
-    total_r.gather()
     total_r.wait()
     for k in range(3):
         right_out[k] = lax.dot_general(
@@ -368,6 +381,7 @@
     count, _, rank = warm_start.shape
     halves = 2 if weight_columns % 256 == 0 else 1
     vmem = pl.BlockSpec(memory_space=pltpu.VMEM)
+    gram_width = pl.cdiv(count * rank, 128) * 128
     loads = 4 + halves + n_dp // n_tp
     left, right = pl.pallas_call(
         functools.partial(kernel, n_dp, n_tp),
@@ -383,12 +397,14 @@
             pltpu.VMEM(up_pre.shape, BF16),
             pltpu.VMEM((count, rank, own), F32),
             pltpu.SemaphoreType.DMA((loads,)),
-            pltpu.VMEM((n_dp, halves, hidden_units, weight_columns // halves), BF16),
+            pltpu.VMEM((n_dp, hidden_units, weight_columns), BF16),
             pltpu.SemaphoreType.DMA((n_dp, halves)),
             pltpu.SemaphoreType.DMA((n_dp, halves)),
             pltpu.VMEM((n_dp, tokens, weight_columns), BF16),
             pltpu.SemaphoreType.DMA((2, n_tp - 1)),
             pltpu.SemaphoreType.DMA((2, n_tp - 1)),
+            pltpu.VMEM((tokens, hidden_units), F32),
+            pltpu.VMEM((tokens, hidden_units), F32),
             pltpu.VMEM((tokens, hidden_units), F32),
             pltpu.VMEM((tokens, hidden_units), BF16),
             pltpu.VMEM((tokens, hidden_units), BF16),
@@ -397,8 +413,8 @@
             *exchange_scratch(n_dp, count * rank, hidden_units),
             *exchange_scratch(n_tp, count * rank, tokens),
             *exchange_scratch(n_dp, count * rank, own),
-            pltpu.VMEM((count, rank, rank), F32),
-            pltpu.VMEM((n_tp - 1, count, rank, rank), F32),
+            pltpu.VMEM((rank, gram_width), F32),
+            pltpu.VMEM((n_tp - 1, rank, gram_width), F32),
             pltpu.SemaphoreType.DMA((2, n_tp - 1)),
         ],
         compiler_params=pltpu.CompilerParams(

time: 94.9 us -> 87.2 us (0.919)
  Pallas kernels: 91 us -> 83.3 us
    pallas_call x1, Pallas kernels: 91 us -> 83.3 us  [shards(): pl.pallas_call(functools.partial(kernel, n_dp, n_tp), out_shape=(jax.Shap...]
where the time goes in v3:
time: 87.2 us; the launch traced here: 86.5 us
  Pallas kernels  83.3 us (96%)
  local copies, waits for them, and re-layouts  2.53 us (3%)
    pallas_call x1, Pallas kernels, shards(): pl.pallas_call(functools.partial(kernel, n_dp, n_tp), out_shape=(jax.Shap...  83.3 us
    unnamed x4, local copies, waits for them, and re-layouts  2.53 us

profile of v3, /device:TPU:0, one launch (start us, length us, event | category | flops | bytes accessed | tf_op | source)
XLA Modules:
  0.0 86.5 jit_solution(10695412801709201375)
XLA Ops:
  0.6 83.3 %powersgd.1 = (f32[3,32,896]{2,1,0:T(8,128)}, f32[3,32,1024]{2,1,0:T(8,128)}) custom-call(bf16[256,1024]{1,0:T(8,128)(2,1)} %x_hbm.1, bf16[256,1024]{1,0:T(8,128)(2,1)} %g_hbm.1, bf16[256,896]{1,0:T(8,128)(2,1)} %gate_hbm.1, bf16[256,896]{1,0:T(8,128)(2,1)} %up_hbm.1, bf16[896,512]{1,0:T(8,128)(2,1)} %w_hbm.1, f32[3,32,1024]{2,1,0:T(8,128)} %bitcast.3), custom_call_target="tpu_custom_call" | custom-call | tf_op jit(solution)/shard_map/powersgd/pallas_call | solution.py:386
  83.9 0.0 copy-start
  83.9 1.8 %copy.10 = f32[3,896,32]{1,2,0:T(8,128)} copy(f32[3,896,32]{1,2,0:T(8,128)} %bitcast.5) | data formatting | bytes 688128
  85.7 0.0 copy-done
  85.7 0.7 copy.11
Async XLA Ops:
  83.9 1.8 %copy-start = (f32[3,32,1024]{2,1,0:T(8,128)S(1)}, f32[3,32,1024]{2,1,0:T(8,128)}, u32[]{:S(2)}) copy-start(f32[3,32,1024]{2,1,0:T(8,128)} %get-tuple-element.5) | copy-start | bytes 1179652

commit v4 on v3

--- a/solution.py
+++ b/solution.py
@@ -133,8 +133,7 @@
 
 def kernel(n_dp, n_tp, x_hbm, g_hbm, gate_hbm, up_hbm, w_hbm, warm_hbm, left_out, right_out,
            x_ref, gate_ref, up_ref, warm_ref, load_sems, wbuf, wsend, wrecv, gfull, gsend, grecv, hg, gate_slope, up_slope, gate_grad, up_grad, hidden,
-           p0, p1, p2, p3, l0, l1, l2, l3, m0, m1, m2, m3, r0, r1, r2, r3,
-           gram_own, gram_come, gram_sems):
+           gram_own, gram_come, gram_sems, *exchange_refs):
     d, z = lax.axis_index("dp"), lax.axis_index("tensor")
     tokens = x_ref.shape[0]
     rank = warm_ref.shape[1]
@@ -237,7 +236,7 @@
     gram_copies = []
 
     def finish():
-        for exchange in (total_p, total_l, total_m, total_r):
+        for exchange in exchanges:
             exchange.finish()
         for copy in gram_copies + weight_copies:
             copy.wait_send()
@@ -252,10 +251,12 @@
         load_w[half].wait()
         weight_send(0, half, 0)
 
-    total_p = Exchange("tensor", n_tp, (p0, p1, p2, p3))
-    total_l = Exchange("dp", n_dp, (l0, l1, l2, l3))
-    total_m = Exchange("tensor", n_tp, (m0, m1, m2, m3))
-    total_r = Exchange("dp", n_dp, (r0, r1, r2, r3))
+    total_p, left_pair, left_last, mid_pair, mid_last, right_pair, right_last = exchanges = [
+        Exchange(axis, count, exchange_refs[4 * index : 4 * index + 4])
+        for index, (axis, count) in enumerate(
+            [("tensor", n_tp)] + [("dp", n_dp)] * 2 + [("tensor", n_tp)] * 2 + [("dp", n_dp)] * 2
+        )
+    ]
     lefts = (gate_grad, up_grad, hidden)
 
     def right(k):
@@ -305,10 +306,17 @@
     for position in waves:
         weight_wave(position)
     total_p.wait()
+
+    def left_part(k):
+        return exact_dot(total_p.load(k * rank, rank), lefts[k][...], NN) * (1.0 / tokens)
+
+    left_last.store(0, left_part(2))
+    left_last.scatter()
     weight_wave(bits - 1)
     hg[...] = product(z)
     for hop in range(last):
         line_use(hop)
+    left_last.gather()
     line_wait(last)
     line_use(last)
 
@@ -316,18 +324,25 @@
     gate_grad[...] = (hidden_grad * gate_slope[...]).astype(BF16)
     up_grad[...] = (hidden_grad * up_slope[...]).astype(BF16)
 
-    for k in range(3):
-        total_l.store(k * rank, exact_dot(total_p.load(k * rank, rank), lefts[k][...], NN) * (1.0 / tokens))
-    total_l.scatter()
-    total_l.gather()
-    total_l.wait()
-
+    for k in range(2):
+        left_pair.store(k * rank, left_part(k))
+    left_pair.scatter()
+
+    left_last.wait()
+    mid_last.store(0, exact_dot(left_last.load(0, rank), hidden[...], NT))
+    mid_last.scatter()
+    left_pair.gather()
+    mid_last.gather()
+    left_pair.wait()
+    raws = [left_pair.load(0, rank), left_pair.load(rank, rank), left_last.load(0, rank)]
+    for k in range(2):
+        mid_pair.store(k * rank, exact_dot(raws[k], lefts[k][...], NT))
+    mid_pair.scatter()
     gram_own[...] = jnp.zeros_like(gram_own)
     for k in range(3):
-        raw = total_l.load(k * rank, rank)
-        total_m.store(k * rank, exact_dot(raw, lefts[k][...], NT))
-        gram_own[:, k * rank : (k + 1) * rank] = lax.dot_general(raw, raw, NT, precision=HIGH, preferred_element_type=F32)
-    total_m.scatter()
+        gram_own[:, k * rank : (k + 1) * rank] = lax.dot_general(
+            raws[k], raws[k], NT, precision=HIGH, preferred_element_type=F32
+        )
     for step in range(1, n_tp):
         copy = pltpu.make_async_remote_copy(
             src_ref=gram_own, dst_ref=gram_come.at[step - 1],
@@ -336,12 +351,16 @@
         )
         copy.start()
         gram_copies.append(copy)
-    total_m.gather()
-    total_m.wait()
-
-    for k in range(3):
-        total_r.store(k * rank, exact_dot(total_m.load(k * rank, rank), right(k), NN))
-    total_r.scatter()
+
+    mid_last.wait()
+    right_last.store(0, exact_dot(mid_last.load(0, rank), right(2), NN))
+    right_last.scatter()
+    mid_pair.gather()
+    right_last.gather()
+    mid_pair.wait()
+    for k in range(2):
+        right_pair.store(k * rank, exact_dot(mid_pair.load(k * rank, rank), right(k), NN))
+    right_pair.scatter()
 
     gram = gram_own[:, : 3 * rank]
     for step in range(1, n_tp):
@@ -350,17 +369,18 @@
     inverse = inverse_cholesky(
         jnp.stack([gram[:, k * rank : (k + 1) * rank] for k in range(3)])
     )
-    total_r.gather()
+    right_pair.gather()
+
+    def orthogonal(k, raw):
+        return lax.dot_general(inverse[k], raw, NN, precision=HIGH, preferred_element_type=F32)
+
     for k in range(3):
-        left_out[k] = lax.dot_general(
-            inverse[k], total_l.load(k * rank, rank), NN, precision=HIGH, preferred_element_type=F32
-        )
-
-    total_r.wait()
-    for k in range(3):
-        right_out[k] = lax.dot_general(
-            inverse[k], total_r.load(k * rank, rank), NN, precision=HIGH, preferred_element_type=F32
-        ) * (1.0 / (tokens * n_dp))
+        left_out[k] = orthogonal(k, raws[k])
+    right_last.wait()
+    right_out[2] = orthogonal(2, right_last.load(0, rank)) * (1.0 / (tokens * n_dp))
+    right_pair.wait()
+    for k in range(2):
+        right_out[k] = orthogonal(k, right_pair.load(k * rank, rank)) * (1.0 / (tokens * n_dp))
 
     finish()
 
@@ -409,13 +429,16 @@
             pltpu.VMEM((tokens, hidden_units), BF16),
             pltpu.VMEM((tokens, hidden_units), BF16),
             pltpu.VMEM((tokens, hidden_units), BF16),
-            *exchange_scratch(n_tp, count * rank, tokens),
-            *exchange_scratch(n_dp, count * rank, hidden_units),
-            *exchange_scratch(n_tp, count * rank, tokens),
-            *exchange_scratch(n_dp, count * rank, own),
             pltpu.VMEM((rank, gram_width), F32),
             pltpu.VMEM((n_tp - 1, rank, gram_width), F32),
             pltpu.SemaphoreType.DMA((2, n_tp - 1)),
+            *exchange_scratch(n_tp, 3 * rank, tokens),
+            *exchange_scratch(n_dp, 2 * rank, hidden_units),
+            *exchange_scratch(n_dp, rank, hidden_units),
+            *exchange_scratch(n_tp, 2 * rank, tokens),
+            *exchange_scratch(n_tp, rank, tokens),
+            *exchange_scratch(n_dp, 2 * rank, own),
+            *exchange_scratch(n_dp, rank, own),
         ],
         compiler_params=pltpu.CompilerParams(
             collective_id=0, has_side_effects=True, vmem_limit_bytes=56 * 1024 * 1024

time: 87.2 us -> 78.2 us (0.90)
  Pallas kernels: 83.3 us -> 74.9 us
    pallas_call x1, Pallas kernels: 83.3 us -> 74.9 us  [shards(): pl.pallas_call(functools.partial(kernel, n_dp, n_tp), out_shape=(jax.Shap...]
where the time goes in v4:
time: 78.2 us; the launch traced here: 78.1 us
  Pallas kernels  74.9 us (96%)
  local copies, waits for them, and re-layouts  2.53 us (3%)
    pallas_call x1, Pallas kernels, shards(): pl.pallas_call(functools.partial(kernel, n_dp, n_tp), out_shape=(jax.Shap...  74.9 us
    unnamed x4, local copies, waits for them, and re-layouts  2.53 us

profile of v4, /device:TPU:0, one launch (start us, length us, event | category | flops | bytes accessed | tf_op | source)
XLA Modules:
  0.0 78.1 jit_solution(17688047347105109361)
XLA Ops:
  0.6 74.9 %powersgd.1 = (f32[3,32,896]{2,1,0:T(8,128)}, f32[3,32,1024]{2,1,0:T(8,128)}) custom-call(bf16[256,1024]{1,0:T(8,128)(2,1)} %x_hbm.1, bf16[256,1024]{1,0:T(8,128)(2,1)} %g_hbm.1, bf16[256,896]{1,0:T(8,128)(2,1)} %gate_hbm.1, bf16[256,896]{1,0:T(8,128)(2,1)} %up_hbm.1, bf16[896,512]{1,0:T(8,128)(2,1)} %w_hbm.1, f32[3,32,1024]{2,1,0:T(8,128)} %bitcast.3), custom_call_target="tpu_custom_call" | custom-call | tf_op jit(solution)/shard_map/powersgd/pallas_call | solution.py:406
  75.5 0.0 copy-start
  75.6 1.8 %copy.10 = f32[3,896,32]{1,2,0:T(8,128)} copy(f32[3,896,32]{1,2,0:T(8,128)} %bitcast.5) | data formatting | bytes 688128
  77.3 0.0 copy-done
  77.3 0.7 copy.11
Async XLA Ops:
  75.5 1.8 %copy-start = (f32[3,32,1024]{2,1,0:T(8,128)S(1)}, f32[3,32,1024]{2,1,0:T(8,128)}, u32[]{:S(2)}) copy-start(f32[3,32,1024]{2,1,0:T(8,128)} %get-tuple-element.5) | copy-start | bytes 1179652

commit v5 on v4

--- a/solution.py
+++ b/solution.py
@@ -36,23 +36,28 @@
     return out[:rows] + (out[rows : 2 * rows] + out[2 * rows :])
 
 
-def inverse_cholesky(gram):
-    count, rank, _ = gram.shape
-    row_id = lax.broadcasted_iota(jnp.int32, (count, rank, rank), 1)
-    col_id = lax.broadcasted_iota(jnp.int32, (count, rank, rank), 2)
-    work = jnp.concatenate([(row_id == col_id).astype(F32), gram], axis=2)
-    row_wide = lax.broadcasted_iota(jnp.int32, work.shape, 1)
-    scale = jnp.zeros((count, rank, 1), F32)
-    row_thin = lax.broadcasted_iota(jnp.int32, scale.shape, 1)
-    for step in range(rank):
-        row = work[:, step : step + 1, :]
-        pivot = work[:, step : step + 1, rank + step : rank + step + 1]
-        scale = jnp.where(row_thin == step, lax.rsqrt(pivot), scale)
-        if step < rank - 1:
-            column = work[:, :, rank + step : rank + step + 1]
-            factor = column / pivot
-            work = work - jnp.where(row_wide > step, factor * row, 0.0)
-    return work[:, :, :rank] * scale
+class InverseCholesky:
+    def __init__(self, gram):
+        count, self.rank, _ = gram.shape
+        row_id = lax.broadcasted_iota(jnp.int32, gram.shape, 1)
+        col_id = lax.broadcasted_iota(jnp.int32, gram.shape, 2)
+        self.work = jnp.concatenate([(row_id == col_id).astype(F32), gram], axis=2)
+        self.row_wide = lax.broadcasted_iota(jnp.int32, self.work.shape, 1)
+        self.scale = jnp.zeros((count, self.rank, 1), F32)
+        self.row_thin = lax.broadcasted_iota(jnp.int32, self.scale.shape, 1)
+
+    def run(self, first, end):
+        for step in range(first, end):
+            at = self.rank + step
+            row = self.work[:, step : step + 1, :]
+            pivot = self.work[:, step : step + 1, at : at + 1]
+            self.scale = jnp.where(self.row_thin == step, lax.rsqrt(pivot), self.scale)
+            if step < self.rank - 1:
+                factor = self.work[:, :, at : at + 1] / pivot
+                self.work = self.work - jnp.where(self.row_wide > step, factor * row, 0.0)
+
+    def result(self):
+        return self.work[:, :, : self.rank] * self.scale
 
 
 class Exchange:
@@ -171,39 +176,36 @@
         copy.wait()
     pl.semaphore_wait(barrier, n_dp - 1 + n_tp - 1)
 
-    def shard(index):
-        return gfull.at[pl.ds(index * per, per)]
-
-    def line_copy(way, hop):
-        source = z - hop if way == 0 else z + hop
-        target = z + 1 if way == 0 else z - 1
+    def line_copy(way, hop, part, source, target):
+        place = gfull.at[source * per + part]
         return pltpu.make_async_remote_copy(
-            src_ref=shard(source), dst_ref=shard(source),
-            send_sem=gsend.at[way, hop], recv_sem=grecv.at[way, hop],
+            src_ref=place, dst_ref=place,
+            send_sem=gsend.at[way, hop, part], recv_sem=grecv.at[way, hop, part],
             device_id={"tensor": target}, device_id_type=MESH,
         )
+
+    def line_out(way, hop, part):
+        if way == 0:
+            return line_copy(way, hop, part, z - hop, z + 1)
+        return line_copy(way, hop, part, z + hop, z - 1)
 
     def line_sends(way, hop):
         if way == 0:
             return jnp.logical_and(z - hop >= 0, z < n_tp - 1)
         return jnp.logical_and(z + hop <= n_tp - 1, z > 0)
 
-    def line_start(hop):
+    def line_start(hop, part):
         for way in (0, 1):
             @pl.when(line_sends(way, hop))
             def _():
-                line_copy(way, hop).start()
-
-    def line_wait(hop):
+                line_out(way, hop, part).start()
+
+    def line_wait(hop, part):
         for way in (0, 1):
             source = z - 1 - hop if way == 0 else z + 1 + hop
             @pl.when(source >= 0 if way == 0 else source <= n_tp - 1)
             def _():
-                pltpu.make_async_remote_copy(
-                    src_ref=shard(source), dst_ref=shard(source),
-                    send_sem=gsend.at[way, hop], recv_sem=grecv.at[way, hop],
-                    device_id={"tensor": z - 1 if way == 0 else z + 1}, device_id_type=MESH,
-                ).wait_recv()
+                line_copy(way, hop, part, source, z - 1 if way == 0 else z + 1).wait_recv()
 
     orders = [list(range(1, bits)) + [0], list(range(bits - 1, 0, -1)) + [0]]
     weight_copies = []
@@ -244,9 +246,11 @@
             for way in (0, 1):
                 @pl.when(line_sends(way, hop))
                 def _():
-                    line_copy(way, hop).wait_send()
-
-    line_start(0)
+                    for part in range(per):
+                        line_out(way, hop, part).wait_send()
+
+    for part in range(per):
+        line_start(0, part)
     for half in range(halves):
         load_w[half].wait()
         weight_send(0, half, 0)
@@ -279,28 +283,29 @@
     gate_slope[...] = up * sigma * (1.0 + gate * (1.0 - sigma))
     up_slope[...] = gate * sigma
 
-    def product(source):
+    def product(source, parts):
         total = None
-        for part in range(per):
+        for part in parts:
             block = source * per + part
             term = lax.dot_general(gfull[block], wbuf[block], NT, preferred_element_type=F32)
             total = term if total is None else total + term
         return total
 
-    def line_use(hop):
+    def line_use(hop, parts):
         for way in (0, 1):
             source = z - 1 - hop if way == 0 else z + 1 + hop
             @pl.when(source >= 0 if way == 0 else source <= n_tp - 1)
             def _():
-                hg[...] += product(source)
+                hg[...] += product(source, parts)
 
     last = n_tp - 2
     waves = list(range(bits - 1))
     for hop in range(last):
-        line_wait(hop)
-        line_start(hop + 1)
-        if waves:
-            weight_wave(waves.pop(0))
+        for part in range(per):
+            line_wait(hop, part)
+            line_start(hop + 1, part)
+            if part == per - 1 and waves:
+                weight_wave(waves.pop(0))
         if hop == 0:
             total_p.gather()
     for position in waves:
@@ -313,12 +318,13 @@
     left_last.store(0, left_part(2))
     left_last.scatter()
     weight_wave(bits - 1)
-    hg[...] = product(z)
+    hg[...] = product(z, range(per))
     for hop in range(last):
-        line_use(hop)
+        line_use(hop, range(per))
     left_last.gather()
-    line_wait(last)
-    line_use(last)
+    for part in range(per):
+        line_wait(last, part)
+        line_use(last, [part])
 
     hidden_grad = hg[...]
     gate_grad[...] = (hidden_grad * gate_slope[...]).astype(BF16)
@@ -357,19 +363,23 @@
     right_last.scatter()
     mid_pair.gather()
     right_last.gather()
+    gram = gram_own[:, : 3 * rank]
+    for step in range(1, n_tp):
+        gram_copies[step - 1].wait_recv()
+        gram = gram + gram_come[step - 1, :, : 3 * rank]
+    cholesky = InverseCholesky(
+        jnp.stack([gram[:, k * rank : (k + 1) * rank] for k in range(3)])
+    )
+    cholesky.run(0, rank // 4)
     mid_pair.wait()
     for k in range(2):
         right_pair.store(k * rank, exact_dot(mid_pair.load(k * rank, rank), right(k), NN))
     right_pair.scatter()
 
-    gram = gram_own[:, : 3 * rank]
-    for step in range(1, n_tp):
-        gram_copies[step - 1].wait_recv()
-        gram = gram + gram_come[step - 1, :, : 3 * rank]
-    inverse = inverse_cholesky(
-        jnp.stack([gram[:, k * rank : (k + 1) * rank] for k in range(3)])
-    )
+    cholesky.run(rank // 4, 3 * rank // 4)
     right_pair.gather()
+    cholesky.run(3 * rank // 4, rank)
+    inverse = cholesky.result()
 
     def orthogonal(k, raw):
         return lax.dot_general(inverse[k], raw, NN, precision=HIGH, preferred_element_type=F32)
@@ -421,8 +431,8 @@
             pltpu.SemaphoreType.DMA((n_dp, halves)),
             pltpu.SemaphoreType.DMA((n_dp, halves)),
             pltpu.VMEM((n_dp, tokens, weight_columns), BF16),
-            pltpu.SemaphoreType.DMA((2, n_tp - 1)),
-            pltpu.SemaphoreType.DMA((2, n_tp - 1)),
+            pltpu.SemaphoreType.DMA((2, n_tp - 1, n_dp // n_tp)),
+            pltpu.SemaphoreType.DMA((2, n_tp - 1, n_dp // n_tp)),
             pltpu.VMEM((tokens, hidden_units), F32),
             pltpu.VMEM((tokens, hidden_units), F32),
             pltpu.VMEM((tokens, hidden_units), F32),

time: 78.2 us -> 78.2 us (level)
  no operation moved by 1% of the time
where the time goes in v5:
time: 78.2 us; the launch traced here: 78.1 us
  Pallas kernels  74.9 us (96%)
  local copies, waits for them, and re-layouts  2.53 us (3%)
    pallas_call x1, Pallas kernels, shards(): pl.pallas_call(functools.partial(kernel, n_dp, n_tp), out_shape=(jax.Shap...  74.9 us
    unnamed x4, local copies, waits for them, and re-layouts  2.53 us

profile of v5, /device:TPU:0, one launch (start us, length us, event | category | flops | bytes accessed | tf_op | source)
XLA Modules:
  0.0 78.1 jit_solution(7683819050708635476)
XLA Ops:
  0.6 74.9 %powersgd.1 = (f32[3,32,896]{2,1,0:T(8,128)}, f32[3,32,1024]{2,1,0:T(8,128)}) custom-call(bf16[256,1024]{1,0:T(8,128)(2,1)} %x_hbm.1, bf16[256,1024]{1,0:T(8,128)(2,1)} %g_hbm.1, bf16[256,896]{1,0:T(8,128)(2,1)} %gate_hbm.1, bf16[256,896]{1,0:T(8,128)(2,1)} %up_hbm.1, bf16[896,512]{1,0:T(8,128)(2,1)} %w_hbm.1, f32[3,32,1024]{2,1,0:T(8,128)} %bitcast.3), custom_call_target="tpu_custom_call" | custom-call | tf_op jit(solution)/shard_map/powersgd/pallas_call | solution.py:416
  75.5 0.0 copy-start
  75.5 1.8 %copy.10 = f32[3,896,32]{1,2,0:T(8,128)} copy(f32[3,896,32]{1,2,0:T(8,128)} %bitcast.5) | data formatting | bytes 688128
  77.3 0.0 copy-done
  77.3 0.7 copy.11
Async XLA Ops:
  75.5 1.8 %copy-start = (f32[3,32,1024]{2,1,0:T(8,128)S(1)}, f32[3,32,1024]{2,1,0:T(8,128)}, u32[]{:S(2)}) copy-start(f32[3,32,1024]{2,1,0:T(8,128)} %get-tuple-element.5) | copy-start | bytes 1179652
